TPU v7x, 32 devices: a whole 2x2x4 slice. The times are simulated.
32 devices in a mesh: energy: 2 (over x), mom: 16 (over z, y, core).
Axes of the slice: x: 2, y: 2, z: 4, core: 2. Of those that a mesh axis runs over, the one named last changes fastest.
Arguments:
- source: float32 [256, 128, 1024], P(('energy', 'mom')), parts along dimension 0, may hold values from -6 to 6
- green: float32 [256, 1024], P(('energy', 'mom')), parts along dimension 0, may hold values from 0.1 to 0.6
- couple_one: float32 [2, 4, 128, 128], replicated, may hold values from -0.5 to 0.5
- couple_two: float32 [2, 4, 128, 128], replicated, may hold values from -0.5 to 0.5
- p_bracket: int32 [2, 1024], replicated, may hold values from 0 to 28
- q_bracket: int32 [2, 1024], replicated, may hold values from 0 to 28
- p_weight: float32 [2, 4, 1024], replicated, may hold values from -0.25 to 1
- q_weight: float32 [2, 4, 1024], replicated, may hold values from -0.25 to 1
- qr_bracket: int32 [2, 1024], replicated, may hold values from 0 to 28
- r_bracket: int32 [2, 1024], replicated, may hold values from 0 to 28
- qr_weight: float32 [2, 4, 1024], replicated, may hold values from -0.25 to 1
- r_weight: float32 [2, 4, 1024], replicated, may hold values from -0.25 to 1
Outputs:
- amplitude: float32 [256, 128, 1024], P(('energy', 'mom')), parts along dimension 0
- component: float32 [256, 128, 1024], P(('energy', 'mom')), parts along dimension 0
There are 2 independent parts, one for each index of `energy`. A program takes and returns all parts, laid end to end along the dimension named above; an argument that names none is the same for every part. Nothing has to cross between parts.
All inputs are finite; a program needn't handle non-finite values.
Results may differ from a plain program's by a relative error of at most 0.0001.
Values sent between devices are 32-bit elements; how exact they have to be, the bound alone decides.
A program may use at most 128 MiB of HBM per device.

v0:
```python
import jax
import jax.numpy as jnp
from jax import lax
from jax.sharding import PartitionSpec as P

P_SIZE = 32
Q = 32
R = 32
K = 2
ITERS = 2


def spline_matrix(
    first_index, second_index, first_weight, second_weight, first_count, second_count
):
    first_grid = jnp.arange(first_count, dtype=jnp.int32)[None, :] - first_index[:, None]
    second_grid = jnp.arange(second_count, dtype=jnp.int32)[None, :] - second_index[:, None]
    first_rows = jnp.zeros(first_grid.shape, jnp.float32)
    second_rows = jnp.zeros(second_grid.shape, jnp.float32)
    for offset in range(4):
        first_rows = first_rows + jnp.where(
            first_grid == offset, first_weight[offset][:, None], jnp.float32(0.0)
        )
        second_rows = second_rows + jnp.where(
            second_grid == offset, second_weight[offset][:, None], jnp.float32(0.0)
        )
    return (first_rows[:, :, None] * second_rows[:, None, :]).reshape(
        first_index.shape[0], first_count * second_count
    )


def class_mats(couple, row_count, start):
    classes = (start + jnp.arange(row_count, dtype=jnp.int32)) % 4
    select = jax.nn.one_hot(classes, 4, dtype=jnp.float32)
    return jnp.einsum("rc,cmn->rmn", select, couple, precision=lax.Precision.HIGHEST)


def mix(mats, values):
    return jnp.einsum("rmn,rnx->rmx", mats, values, precision=lax.Precision.HIGHEST)


def interp(values, smat):
    return jnp.einsum("rcx,yx->rcy", values, smat, precision=lax.Precision.HIGHEST)


def to_send_one(values, quarter):
    rows = values.shape[0]
    return (
        values.reshape(rows, 4, quarter, P_SIZE, Q)
        .transpose(3, 1, 0, 2, 4)
        .reshape(4 * P_SIZE, rows, quarter * Q)
    )


def from_send_one(arrived, quarter):
    rows = arrived.shape[0]
    return (
        arrived.reshape(rows, R, 4, quarter, Q)
        .transpose(0, 3, 2, 4, 1)
        .reshape(rows, 4 * quarter, Q * R)
    )


def to_send_two(values, quarter):
    rows = values.shape[0]
    return (
        values.reshape(rows, quarter, 4, Q, R)
        .transpose(4, 2, 0, 1, 3)
        .reshape(4 * R, rows, quarter * Q)
    )


def from_send_two(arrived, quarter):
    rows = arrived.shape[0]
    return (
        arrived.reshape(rows, P_SIZE, 4, quarter, Q)
        .transpose(0, 2, 3, 1, 4)
        .reshape(rows, 4 * quarter, P_SIZE * Q)
    )


def shards(
    source,
    green,
    couple_one,
    couple_two,
    p_bracket,
    q_bracket,
    p_weight,
    q_weight,
    qr_bracket,
    r_bracket,
    qr_weight,
    r_weight,
):
    rows_one = source.shape[0]
    rows_two = green.shape[0]
    quarter = source.shape[1] // 4
    here = lax.axis_index("mom")
    first_maps = [
        spline_matrix(p_bracket[k], q_bracket[k], p_weight[k], q_weight[k], P_SIZE, Q)
        for k in range(K)
    ]
    second_maps = [
        spline_matrix(qr_bracket[k], r_bracket[k], qr_weight[k], r_weight[k], Q, R)
        for k in range(K)
    ]
    mats_one = [class_mats(couple_one[k], rows_one, here * rows_one) for k in range(K)]
    mats_two = [class_mats(couple_two[k], rows_two, here * rows_two) for k in range(K)]
    scale = green[:, None, :]
    state = source
    component = None
    for step in range(ITERS):
        one = interp(mix(mats_one[0], state), first_maps[0])
        k = 1
        one = one + interp(mix(mats_one[k], state), first_maps[k])
        arrived = lax.all_to_all(
            to_send_one(one, quarter), "mom", split_axis=0, concat_axis=1, tiled=True
        )
        regrouped = from_send_one(arrived, quarter)
        total = mix(mats_two[0], interp(regrouped, second_maps[0]))
        k = 1
        total = total + mix(mats_two[k], interp(regrouped, second_maps[k]))
        component = scale * total
        returned = lax.all_to_all(
            to_send_two(component, quarter), "mom", split_axis=0, concat_axis=1, tiled=True
        )
        state = source + from_send_two(returned, quarter)
    return (state, component)


def solution(mesh):
    placed = (
        P(("energy", "mom"), None, None),
        P(("energy", "mom"), None),
        P(),
        P(),
        P(),
        P(),
        P(),
        P(),
        P(),
        P(),
        P(),
        P(),
    )
    return jax.shard_map(
        shards,
        mesh=mesh,
        in_specs=placed,
        out_specs=(P(("energy", "mom"), None, None), P(("energy", "mom"), None, None)),
        check_vma=False,
    )
```

profile of v0, /device:TPU:31, one launch (start us, length us, event | category | flops | bytes accessed | tf_op | source)
XLA Modules:
  0.0 921.9 jit_solution(14042595359069601299)
XLA Ops:
  6.3 5.8 fusion.8
  12.2 4.1 fusion.14
  17.6 14.4 %fusion.68 = f32[8,128,1024]{2,1,0:T(8,128)S(1)} fusion(f32[8,128,1024]{2,1,0:T(8,128)S(1)} %fusion.8, f32[1024,1024,1]{0,1,2:T(8,128)S(1)} %bitcast.165), kind=kOutput, calls=%fused_computation.102 | convolution fusion | flops 12884901888 | bytes 12582912 | tf_op jit(solution)/shard_map/rcx,yx->rcy/dot_general | solution.py:43
  31.9 14.8 %convolution_add_fusion.1 = f32[8,128,1024]{2,1,0:T(8,128)} fusion(f32[8,128,1024]{2,1,0:T(8,128)S(1)} %fusion.68, f32[8,128,1024]{2,1,0:T(8,128)S(1)} %fusion.14, f32[1024,1024,1]{0,1,2:T(8,128)S(1)} %bitcast.156), kind=kOutput, calls=%fused_computation.13 | convolution fusion | flops 12885950464 | bytes 16777216 | tf_op jit(solution)/shard_map/rcx,yx->rcy/dot_general | solution.py:43
  46.8 11.6 %reshape.954 = f32[8,4,32,32,32]{4,3,2,1,0:T(8,128)} reshape(f32[8,128,1024]{2,1,0:T(8,128)} %convolution_add_fusion.1) | data formatting | bytes 8388608 | tf_op jit(solution)/shard_map/reshape | solution.py:49
  58.4 14.3 %copy.127 = f32[8,4,32,32,32]{4,2,0,1,3:T(8,128)} copy(f32[8,4,32,32,32]{4,3,2,1,0:T(8,128)} %reshape.954) | data formatting | bytes 8388608 | tf_op jit(solution)/shard_map/reshape | solution.py:49
  72.7 13.7 %reshape.955 = f32[128,8,1024]{2,1,0:T(8,128)} reshape(f32[32,4,8,32,32]{4,3,2,1,0:T(8,128)} %bitcast.148) | data formatting | bytes 8388608 | tf_op jit(solution)/shard_map/reshape | solution.py:51
  86.4 6.5 all-to-all-start
  96.9 2.6 broadcast_multiply_fusion
  99.5 84.8 %all-to-all-done = f32[128,8,1024]{2,1,0:T(8,128)} async-done(((f32[128,8,1024]{2,1,0:T(8,128)}), f32[128,8,1024]{2,1,0:T(8,128)}, u32[]{:S(2)}, u32[]{:S(2)}) %all-to-all-start) | async-done | bytes 4194336 | tf_op jit(solution)/shard_map/all_to_all | solution.py:117
  184.4 4.8 copy.131
  189.1 11.6 %reshape.956 = f32[8,32,4,32,32]{4,3,2,1,0:T(8,128)} reshape(f32[8,16,8,1024]{3,2,1,0:T(8,128)} %bitcast.158) | data formatting | bytes 8388608 | tf_op jit(solution)/shard_map/reshape | solution.py:58
  200.8 18.9 %copy.53 = f32[8,32,4,32,32]{4,3,2,1,0:T(8,128)} copy(f32[8,32,4,32,32]{3,1,2,4,0:T(8,128)} %bitcast.149) | data formatting | bytes 8388608 | tf_op jit(solution)/shard_map/transpose | solution.py:59
  219.7 13.7 %reshape.957 = f32[8,128,1024]{2,1,0:T(8,128)} reshape(f32[8,32,4,32,32]{4,3,2,1,0:T(8,128)} %copy.53) | data formatting | bytes 8388608 | tf_op jit(solution)/shard_map/reshape | solution.py:60
  233.3 17.2 %fusion.70 = f32[8,128,1024]{2,1,0:T(8,128)S(1)} fusion(f32[8,128,1024]{2,1,0:T(8,128)} %reshape.957, f32[1024,1024,1]{0,1,2:T(8,128)} %bitcast.169), kind=kOutput, calls=%fused_computation.104 | convolution fusion | flops 12884901888 | bytes 12582912 | tf_op jit(solution)/shard_map/rcx,yx->rcy/dot_general | solution.py:43
  250.6 13.4 %fusion.69 = f32[8,128,1024]{2,1,0:T(8,128)S(1)} fusion(f32[8,128,1024]{2,1,0:T(8,128)S(1)} %copy-done.6, f32[1024,1024,1]{0,1,2:T(8,128)S(1)} %bitcast.167), kind=kOutput, calls=%fused_computation.103 | convolution fusion | flops 12884901888 | bytes 12582912 | tf_op jit(solution)/shard_map/rcx,yx->rcy/dot_general | solution.py:43
  264.1 4.2 fusion.4
  268.3 5.2 add_multiply_fusion.1
  273.5 11.6 %reshape.958 = f32[8,32,4,32,32]{4,3,2,1,0:T(8,128)} reshape(f32[8,128,1024]{2,1,0:T(8,128)} %add_multiply_fusion.1) | data formatting | bytes 8388608 | tf_op jit(solution)/shard_map/reshape | solution.py:67
  285.2 20.0 %copy.59 = f32[8,32,4,32,32]{3,1,0,2,4:T(8,128)} copy(f32[8,32,4,32,32]{4,3,2,1,0:T(8,128)} %reshape.958) | data formatting | bytes 8388608 | tf_op jit(solution)/shard_map/reshape | solution.py:67
  305.1 13.7 %reshape.959 = f32[128,8,1024]{2,1,0:T(8,128)} reshape(f32[32,4,8,32,32]{4,3,2,1,0:T(8,128)} %bitcast.150) | data formatting | bytes 8388608 | tf_op jit(solution)/shard_map/reshape | solution.py:69
  318.8 97.7 %all_to_all.60 = f32[128,8,1024]{2,1,0:T(8,128)S(1)} all-to-all(f32[128,8,1024]{2,1,0:T(8,128)} %reshape.959), channel_id=1, replica_groups=mesh['energy'=2,'mom'=16] {'mom'}, dimensions={0} | all-to-all | bytes 8388608 | tf_op jit(solution)/shard_map/all_to_all | solution.py:125
  418.8 11.6 %reshape.960 = f32[8,32,4,32,32]{4,3,2,1,0:T(8,128)} reshape(f32[8,16,8,1024]{3,2,1,0:T(8,128)} %bitcast.159) | data formatting | bytes 8388608 | tf_op jit(solution)/shard_map/reshape | solution.py:76
  430.5 18.4 %copy.61 = f32[8,4,32,32,32]{4,3,2,1,0:T(8,128)} copy(f32[8,4,32,32,32]{4,2,1,3,0:T(8,128)} %bitcast.151) | data formatting | bytes 8388608 | tf_op jit(solution)/shard_map/transpose | solution.py:77
  448.9 13.7 %reshape.961 = f32[8,128,1024]{2,1,0:T(8,128)} reshape(f32[8,4,32,32,32]{4,3,2,1,0:T(8,128)} %copy.61) | data formatting | bytes 8388608 | tf_op jit(solution)/shard_map/reshape | solution.py:78
  462.6 6.4 fusion
  469.0 3.9 fusion.2
  473.0 14.2 %fusion.71 = f32[8,128,1024]{2,1,0:T(8,128)S(1)} fusion(f32[8,128,1024]{2,1,0:T(8,128)S(1)} %fusion.2, f32[1024,1024,1]{0,1,2:T(8,128)S(1)} %bitcast.166), kind=kOutput, calls=%fused_computation.105 | convolution fusion | flops 12884901888 | bytes 12582912 | tf_op jit(solution)/shard_map/rcx,yx->rcy/dot_general | solution.py:43
  487.2 14.8 %convolution_add_fusion = f32[8,128,1024]{2,1,0:T(8,128)} fusion(f32[8,128,1024]{2,1,0:T(8,128)S(1)} %fusion.71, f32[8,128,1024]{2,1,0:T(8,128)S(1)} %fusion, f32[1024,1024,1]{0,1,2:T(8,128)S(1)} %bitcast.157), kind=kOutput, calls=%fused_computation.12 | convolution fusion | flops 12885950464 | bytes 16777216 | tf_op jit(solution)/shard_map/rcx,yx->rcy/dot_general | solution.py:43
  502.0 11.6 %reshape.962 = f32[8,4,32,32,32]{4,3,2,1,0:T(8,128)} reshape(f32[8,128,1024]{2,1,0:T(8,128)} %convolution_add_fusion) | data formatting | bytes 8388608 | tf_op jit(solution)/shard_map/reshape | solution.py:49
  513.6 14.3 %copy.126 = f32[8,4,32,32,32]{4,2,0,1,3:T(8,128)} copy(f32[8,4,32,32,32]{4,3,2,1,0:T(8,128)} %reshape.962) | data formatting | bytes 8388608 | tf_op jit(solution)/shard_map/reshape | solution.py:49
  527.9 13.7 %reshape.963 = f32[128,8,1024]{2,1,0:T(8,128)} reshape(f32[32,4,8,32,32]{4,3,2,1,0:T(8,128)} %bitcast.152) | data formatting | bytes 8388608 | tf_op jit(solution)/shard_map/reshape | solution.py:51
  541.5 97.6 %all_to_all.61 = f32[128,8,1024]{2,1,0:T(8,128)S(1)} all-to-all(f32[128,8,1024]{2,1,0:T(8,128)} %reshape.963), channel_id=1, replica_groups=mesh['energy'=2,'mom'=16] {'mom'}, dimensions={0} | all-to-all | bytes 8388608 | tf_op jit(solution)/shard_map/all_to_all | solution.py:117
  641.4 11.6 %reshape.964 = f32[8,32,4,32,32]{4,3,2,1,0:T(8,128)} reshape(f32[8,16,8,1024]{3,2,1,0:T(8,128)} %bitcast.160) | data formatting | bytes 8388608 | tf_op jit(solution)/shard_map/reshape | solution.py:58
  653.0 18.9 %copy.68 = f32[8,32,4,32,32]{4,3,2,1,0:T(8,128)} copy(f32[8,32,4,32,32]{3,1,2,4,0:T(8,128)} %bitcast.153) | data formatting | bytes 8388608 | tf_op jit(solution)/shard_map/transpose | solution.py:59
  671.9 13.7 %reshape.965 = f32[8,128,1024]{2,1,0:T(8,128)} reshape(f32[8,32,4,32,32]{4,3,2,1,0:T(8,128)} %copy.68) | data formatting | bytes 8388608 | tf_op jit(solution)/shard_map/reshape | solution.py:60
  685.6 17.2 %fusion.73 = f32[8,128,1024]{2,1,0:T(8,128)S(1)} fusion(f32[8,128,1024]{2,1,0:T(8,128)} %reshape.965, f32[1024,1024,1]{0,1,2:T(8,128)} %bitcast.170), kind=kOutput, calls=%fused_computation.107 | convolution fusion | flops 12884901888 | bytes 12582912 | tf_op jit(solution)/shard_map/rcx,yx->rcy/dot_general | solution.py:43
  702.9 13.4 %fusion.72 = f32[8,128,1024]{2,1,0:T(8,128)S(1)} fusion(f32[8,128,1024]{2,1,0:T(8,128)S(1)} %copy-done.5, f32[1024,1024,1]{0,1,2:T(8,128)S(1)} %bitcast.168), kind=kOutput, calls=%fused_computation.106 | convolution fusion | flops 12884901888 | bytes 12582912 | tf_op jit(solution)/shard_map/rcx,yx->rcy/dot_general | solution.py:43
  716.3 4.2 fusion.6
  720.6 5.2 add_multiply_fusion
  725.8 11.6 %reshape.966 = f32[8,32,4,32,32]{4,3,2,1,0:T(8,128)} reshape(f32[8,128,1024]{2,1,0:T(8,128)} %add_multiply_fusion) | data formatting | bytes 8388608 | tf_op jit(solution)/shard_map/reshape | solution.py:67
  737.4 20.0 %copy.73 = f32[8,32,4,32,32]{3,1,0,2,4:T(8,128)} copy(f32[8,32,4,32,32]{4,3,2,1,0:T(8,128)} %reshape.966) | data formatting | bytes 8388608 | tf_op jit(solution)/shard_map/reshape | solution.py:67
  757.4 13.7 %reshape.967 = f32[128,8,1024]{2,1,0:T(8,128)} reshape(f32[32,4,8,32,32]{4,3,2,1,0:T(8,128)} %bitcast.154) | data formatting | bytes 8388608 | tf_op jit(solution)/shard_map/reshape | solution.py:69
  771.1 97.7 %all_to_all.62 = f32[128,8,1024]{2,1,0:T(8,128)S(1)} all-to-all(f32[128,8,1024]{2,1,0:T(8,128)} %reshape.967), channel_id=1, replica_groups=mesh['energy'=2,'mom'=16] {'mom'}, dimensions={0} | all-to-all | bytes 8388608 | tf_op jit(solution)/shard_map/all_to_all | solution.py:125
  871.1 11.6 %reshape.968 = f32[8,32,4,32,32]{4,3,2,1,0:T(8,128)} reshape(f32[8,16,8,1024]{3,2,1,0:T(8,128)} %bitcast.161) | data formatting | bytes 8388608 | tf_op jit(solution)/shard_map/reshape | solution.py:76
  882.7 18.4 %copy.75 = f32[8,4,32,32,32]{4,3,2,1,0:T(8,128)} copy(f32[8,4,32,32,32]{4,2,1,3,0:T(8,128)} %bitcast.155) | data formatting | bytes 8388608 | tf_op jit(solution)/shard_map/transpose | solution.py:77
  901.2 13.7 %reshape.969 = f32[8,128,1024]{2,1,0:T(8,128)} reshape(f32[8,4,32,32,32]{4,3,2,1,0:T(8,128)} %copy.75) | data formatting | bytes 8388608 | tf_op jit(solution)/shard_map/reshape | solution.py:78
  914.9 6.8 add.250
  (59 shorter events, 17.9 us)
Async XLA Ops:
  6.3 5.8 copy-start
  16.9 15.0 %copy-start.7 = (f32[1024,32,32]{0,2,1:T(8,128)}, f32[1024,32,32]{0,2,1:T(8,128)S(1)}, u32[]{:S(2)}) copy-start(f32[1024,32,32]{0,2,1:T(8,128)S(1)} %broadcast_multiply_fusion.3) | copy-start | bytes 12582916
  17.5 14.4 %copy-start.3 = (f32[1024,32,32]{0,2,1:T(8,128)}, f32[1024,32,32]{0,2,1:T(8,128)S(1)}, u32[]{:S(2)}) copy-start(f32[1024,32,32]{0,2,1:T(8,128)S(1)} %broadcast_multiply_fusion.2) | copy-start | bytes 12582916
  86.3 6.5 copy-start.15
  86.3 6.5 copy-start.16
  86.3 6.6 copy-start.13
  86.3 6.6 copy-start.14
  86.3 6.9 copy-start.11
  86.4 98.0 %all-to-all-start = ((f32[128,8,1024]{2,1,0:T(8,128)}), f32[128,8,1024]{2,1,0:T(8,128)}, u32[]{:S(2)}, u32[]{:S(2)}) async-start(f32[128,8,1024]{2,1,0:T(8,128)} %reshape.955), calls=%async_computation | async-start | bytes 8388608 | tf_op jit(solution)/shard_map/all_to_all | solution.py:117
  233.3 17.2 %copy-start.6 = (f32[8,128,1024]{2,1,0:T(8,128)S(1)}, f32[8,128,1024]{2,1,0:T(8,128)}, u32[]{:S(2)}) copy-start(f32[8,128,1024]{2,1,0:T(8,128)} %reshape.957) | copy-start | bytes 12582916
  233.3 17.3 %copy-start.9 = (f32[1024,32,32]{0,2,1:T(8,128)S(1)}, f32[1024,32,32]{0,2,1:T(8,128)}, u32[]{:S(2)}) copy-start(f32[1024,32,32]{0,2,1:T(8,128)} %broadcast_multiply_fusion.1) | copy-start | bytes 12582916
  264.0 4.3 copy-start.12
  462.6 6.4 copy-start.1
  462.6 6.4 copy-start.2
  469.0 4.0 copy-start.8
  472.9 14.2 %copy-start.4 = (f32[1024,32,32]{0,2,1:T(8,128)S(1)}, f32[1024,32,32]{0,2,1:T(8,128)}, u32[]{:S(2)}) copy-start(f32[1024,32,32]{0,2,1:T(8,128)} %copy-done.3) | copy-start | bytes 12582916
  685.6 17.2 %copy-start.5 = (f32[8,128,1024]{2,1,0:T(8,128)S(1)}, f32[8,128,1024]{2,1,0:T(8,128)}, u32[]{:S(2)}) copy-start(f32[8,128,1024]{2,1,0:T(8,128)} %reshape.965) | copy-start | bytes 12582916
  685.6 17.3 %copy-start.10 = (f32[1024,32,32]{0,2,1:T(8,128)S(1)}, f32[1024,32,32]{0,2,1:T(8,128)}, u32[]{:S(2)}) copy-start(f32[1024,32,32]{0,2,1:T(8,128)} %broadcast_multiply_fusion.1) | copy-start | bytes 12582916
where the time goes:
time: 932 us; the launch traced here: 922 us
  local copies, waits for them, and re-layouts  362 us (39%)
  blocking collectives  293 us (31%)
  matrix products  161 us (17%)
  waiting for transfers between devices  84.8 us (9%)
  other arithmetic  13.5 us (1%)
    all_to_all x2, blocking collectives, shards(): lax.all_to_all(to_send_two(component, quarter), 'mom', split_axis=0, conc...  195 us
    dot_general x8, matrix products, interp(): jnp.einsum('rcx,yx->rcy', values, smat, precision=lax.Precision.HIGHEST)  120 us
    all_to_all x1, blocking collectives, shards(): lax.all_to_all(to_send_one(one, quarter), 'mom', split_axis=0, concat_axi...  97.6 us
    all_to_all x1, waiting for transfers between devices, shards(): lax.all_to_all(to_send_one(one, quarter), 'mom', split_axis=0, concat_axi...  84.8 us
    reshape x4, local copies, waits for them, and re-layouts, to_send_two(): values.reshape(rows, quarter, 4, Q, R).transpose(4, 2, 0, 1, 3)  63.2 us
    reshape x4, local copies, waits for them, and re-layouts, to_send_one(): values.reshape(rows, 4, quarter, P_SIZE, Q).transpose(3, 1, 0, 2, 4)  51.8 us
    dot_general x8, matrix products, mix(): jnp.einsum('rmn,rnx->rmx', mats, values, precision=lax.Precision.HIGHEST)  39.1 us
    transpose x2, local copies, waits for them, and re-layouts, from_send_one(): return arrived.reshape(rows, R, 4, quarter, Q).transpose(0, 3, 2, 4, 1).r...  37.8 us
  transfers between devices with their start and end apart: 1, of which 1 were waited for; matrix products, arithmetic and copies ran while one was open for 1% of the time, Pallas kernels for 0%

commit v1 on v0

v1 whole, which is shorter than its diff:
```python
import functools

import jax
import jax.numpy as jnp
from jax import lax
from jax.experimental import pallas as pl
from jax.experimental.pallas import tpu as pltpu
from jax.sharding import PartitionSpec as P

K = 2
ITERS = 2
LANES = 128
F32 = jnp.float32
BF16 = jnp.bfloat16


def split(values):
    high = values.astype(BF16)
    return high, (values - high.astype(F32)).astype(BF16)


def dot3(a_high, a_low, b_high, b_low, dims=(((1,), (0,)), ((), ()))):
    mul = functools.partial(lax.dot_general, dimension_numbers=dims, preferred_element_type=F32)
    return mul(a_high, b_high) + (mul(a_high, b_low) + mul(a_low, b_high))


def sweep_kernel(
    n,
    quarter,
    q_size,
    tab_ref,
    green_t_ref,
    green_ref,
    mix_one_ref,
    mix_two_ref,
    mix_nat_ref,
    source_ref,
    amp_ref,
    comp_ref,
    map_high,
    map_low,
    start_t,
    send_buf,
    recv_one,
    recv_two,
    v_high,
    v_low,
    w_high,
    w_low,
    w_keep,
    e_high,
    e_low,
    d_high,
    d_low,
    a_high,
    a_low,
    load_sem,
    send_sem,
    recv_sem,
):
    me = lax.axis_index("mom")
    grid = start_t.shape[1]
    groups = start_t.shape[0]
    local = start_t.shape[2] // LANES
    block = 2 * LANES
    blocks = grid // block
    block_dests = n // blocks
    per_tile = LANES // q_size

    load = pltpu.make_async_copy(source_ref, amp_ref, load_sem)
    load.start()

    barrier = pltpu.get_barrier_semaphore()

    def greet(offset, carry):
        pl.semaphore_signal(
            barrier,
            inc=1,
            device_id={"mom": lax.rem(me + offset, n)},
            device_id_type=pl.DeviceIdType.MESH,
        )
        return carry

    lax.fori_loop(1, n, greet, 0)

    def rows_of(i, size=block):
        return pl.ds(pl.multiple_of(i * size, size), size)

    def build_map(slot):
        base = 10 * slot

        def body(i, carry):
            rows = rows_of(i)
            table = tab_ref[rows, :]

            def col(j):
                return jnp.broadcast_to(table[:, base + j : base + j + 1], (block, LANES))

            first, second = col(0), col(1)
            w_first = [col(2 + j) for j in range(4)]
            w_second = [col(6 + j) for j in range(4)]
            lane = lax.broadcasted_iota(jnp.int32, (block, LANES), 1)
            fine = (lane % q_size).astype(F32) - second
            coarse = (lane // q_size).astype(F32) - first
            zero = jnp.zeros((block, LANES), F32)
            inner = zero
            for j in range(4):
                inner = inner + jnp.where(fine == j, w_second[j], zero)
            for t in range(grid // LANES):
                here = coarse + F32(per_tile * t)
                outer = zero
                for j in range(4):
                    outer = outer + jnp.where(here == j, w_first[j], zero)
                high, low = split(outer * inner)
                map_high[slot, rows, t * LANES : (t + 1) * LANES] = high
                map_low[slot, rows, t * LANES : (t + 1) * LANES] = low
            return carry

        lax.fori_loop(0, blocks, body, 0)

    def copy_of(phase, g, offset):
        dest = lax.rem(me + offset, n)
        into = recv_one if phase == 0 else recv_two
        return pltpu.make_async_remote_copy(
            src_ref=send_buf.at[g, dest],
            dst_ref=into.at[g, me],
            send_sem=send_sem.at[g, offset],
            recv_sem=recv_sem.at[phase, g, offset],
            device_id={"mom": dest},
            device_id_type=pl.DeviceIdType.MESH,
        )

    def start_sends(phase, g):
        def body(offset, carry):
            copy_of(phase, g, offset).start()
            return carry

        lax.fori_loop(1, n, body, 0)
        into = recv_one if phase == 0 else recv_two
        into[g, me] = send_buf[g, me]

    def wait_sends(phase, g):
        def body(offset, carry):
            copy_of(phase, g, offset).wait_send()
            return carry

        lax.fori_loop(1, n, body, 0)

    def wait_recvs(phase, g):
        into = recv_one if phase == 0 else recv_two

        def body(offset, carry):
            origin = lax.rem(me + n - offset, n)
            pltpu.make_async_remote_copy(
                src_ref=send_buf.at[g, origin],
                dst_ref=into.at[g, origin],
                send_sem=send_sem.at[g, offset],
                recv_sem=recv_sem.at[phase, g, offset],
                device_id={"mom": origin},
                device_id_type=pl.DeviceIdType.MESH,
            ).wait_recv()
            return carry

        lax.fori_loop(1, n, body, 0)

    def set_values(values):
        high, low = split(values)
        v_high[...] = high
        v_low[...] = low

    def place(g, i, part, out):
        out = out.reshape(block_dests, local, q_size, LANES)
        dests = pl.ds(i * block_dests, block_dests)
        for other in range(local):
            send_buf[
                g,
                dests,
                part * q_size : (part + 1) * q_size,
                other * LANES : (other + 1) * LANES,
            ] = out[:, other]

    def one_in(it):
        def body(g, carry):
            if it == 0:
                set_values(start_t[g])
            else:
                wait_recvs(1, g)
                set_values(start_t[g] + recv_two[g].reshape(grid, local * LANES))

            def rows_body(i, inner):
                rows = rows_of(i)
                for k in range(K):
                    out = dot3(map_high[k, rows, :], map_low[k, rows, :], v_high[...], v_low[...])
                    high, low = split(out)
                    lanes = pl.ds(pl.multiple_of((k * groups + g) * LANES, LANES), LANES)
                    for part in range(local):
                        w_high[part, rows, lanes] = high[:, part * LANES : (part + 1) * LANES]
                        w_low[part, rows, lanes] = low[:, part * LANES : (part + 1) * LANES]
                return inner

            lax.fori_loop(0, blocks, rows_body, 0)
            return carry

        lax.fori_loop(0, groups, body, 0)

    def one_out(it):
        def body(g, carry):
            if it > 0:
                wait_sends(1, g)

            def rows_body(i, inner):
                rows = rows_of(i)
                for part in range(local):
                    out = dot3(w_high[part, rows, :], w_low[part, rows, :], e_high[g], e_low[g])
                    place(g, i, part, out)
                return inner

            lax.fori_loop(0, blocks, rows_body, 0)
            start_sends(0, g)
            return carry

        lax.fori_loop(0, groups, body, 0)

    def two(it):
        last = it == ITERS - 1

        def body(g, carry):
            wait_recvs(0, g)
            wait_sends(0, g)
            set_values(recv_one[g].reshape(grid, local * LANES))

            def rows_body(i, inner):
                rows = rows_of(i)
                outs = [
                    dot3(
                        map_high[K + k, rows, :], map_low[K + k, rows, :], v_high[...], v_low[...]
                    )
                    for k in range(K)
                ]
                for part in range(local):
                    lanes = slice(part * LANES, (part + 1) * LANES)
                    joined = jnp.concatenate([out[:, lanes] for out in outs], axis=1)
                    high, low = split(joined)
                    mixed = dot3(high, low, d_high[g], d_low[g])
                    place(g, i, part, mixed * green_t_ref[g, rows, part : part + 1])
                    if last:
                        for k in range(K):
                            w_keep[part, k, rows, :] = outs[k][:, lanes]
                return inner

            lax.fori_loop(0, blocks, rows_body, 0)
            start_sends(1, g)
            if last:
                outer = grid // q_size
                for part in range(local):
                    scale = green_ref[pl.ds(part * groups + g, 1), :]
                    for s in range(blocks):
                        step = block // outer
                        joined = jnp.concatenate(
                            [
                                jnp.concatenate(
                                    [
                                        w_keep[part, k, pl.ds(q, outer, stride=q_size), :]
                                        for q in range(s * step, (s + 1) * step)
                                    ],
                                    axis=0,
                                )
                                for k in range(K)
                            ],
                            axis=1,
                        )
                        high, low = split(joined)
                        out = dot3(a_high[g], a_low[g], high, low, (((1,), (1,)), ((), ())))
                        lanes = slice(s * block, (s + 1) * block)
                        comp_ref[part * groups + g, :, lanes] = out * scale[:, lanes]
            return carry

        lax.fori_loop(0, groups, body, 0)

    for k in range(K):
        build_map(k)
    for g in range(groups):
        e_high[g], e_low[g] = split(mix_one_ref[g])
        d_high[g], d_low[g] = split(mix_two_ref[g])
        a_high[g], a_low[g] = split(mix_nat_ref[g])
    load.wait()

    def transpose_in(g, carry):
        chans = pl.ds(pl.multiple_of(g * quarter, quarter), quarter)
        for part in range(local):
            stacked = jnp.concatenate(
                [amp_ref[part * groups + c, chans, :] for c in range(groups)], axis=0
            )
            start_t[g, :, part * LANES : (part + 1) * LANES] = stacked.T
        return carry

    lax.fori_loop(0, groups, transpose_in, 0)

    for it in range(ITERS):
        one_in(it)
        if it == 0:
            pl.semaphore_wait(barrier, n - 1)
        one_out(it)
        if it == 0:
            for k in range(K):
                build_map(K + k)
        two(it)

    def finish(g, carry):
        wait_recvs(1, g)
        total = start_t[g] + recv_two[g].reshape(grid, local * LANES)
        chans = pl.ds(pl.multiple_of(g * quarter, quarter), quarter)
        for part in range(local):
            turned = total[:, part * LANES : (part + 1) * LANES].T
            for c in range(groups):
                amp_ref[part * groups + c, chans, :] = turned[c * quarter : (c + 1) * quarter]
        wait_sends(1, g)
        return carry

    lax.fori_loop(0, groups, finish, 0)


def fused(
    n,
    source,
    green,
    couple_one,
    couple_two,
    p_bracket,
    q_bracket,
    p_weight,
    q_weight,
    qr_bracket,
    r_bracket,
    qr_weight,
    r_weight,
):
    rows, channels, grid = source.shape
    groups = couple_one.shape[1]
    quarter = channels // groups
    local = rows // groups
    r_size = rows * n // groups
    q_size = grid // r_size

    def turn(values):
        lead = values.shape[:-1]
        return jnp.swapaxes(values.reshape(lead + (q_size, r_size)), -1, -2).reshape(values.shape)

    columns = []
    for k in range(K):
        columns += [p_bracket[k][None].astype(F32), q_bracket[k][None].astype(F32), p_weight[k], q_weight[k]]
    for k in range(K):
        columns += [
            turn(r_bracket[k])[None].astype(F32),
            turn(qr_bracket[k])[None].astype(F32),
            turn(r_weight[k]),
            turn(qr_weight[k]),
        ]
    table = jnp.concatenate(columns, axis=0)
    table = jnp.pad(table, ((0, LANES - table.shape[0]), (0, 0))).T
    green_t = turn(green).reshape(local, groups, grid).transpose(1, 2, 0)

    eye = jnp.eye(groups, dtype=bool)[None, None, None, :, None, :, None]
    blocks = couple_one.reshape(K, groups, groups, quarter, groups, quarter).transpose(2, 0, 4, 1, 5, 3)
    mix_one = jnp.where(eye, blocks[:, :, :, :, :, None, :], F32(0.0)).reshape(
        groups, K * groups * channels, channels
    )
    pieces = couple_two.reshape(K, groups, quarter, groups, quarter, groups)
    mix_two = pieces.transpose(1, 0, 5, 4, 3, 2).reshape(groups, K * channels, channels)
    mix_nat = pieces.transpose(1, 2, 3, 0, 5, 4).reshape(groups, channels, K * channels)

    vmem = pl.BlockSpec(memory_space=pltpu.VMEM)
    scratch = [
        pltpu.VMEM((2 * K, grid, grid), BF16),
        pltpu.VMEM((2 * K, grid, grid), BF16),
        pltpu.VMEM((groups, grid, local * LANES), F32),
        pltpu.VMEM((groups, n, local * q_size, local * LANES), F32),
        pltpu.VMEM((groups, n, local * q_size, local * LANES), F32),
        pltpu.VMEM((groups, n, local * q_size, local * LANES), F32),
        pltpu.VMEM((grid, local * LANES), BF16),
        pltpu.VMEM((grid, local * LANES), BF16),
        pltpu.VMEM((local, grid, K * groups * LANES), BF16),
        pltpu.VMEM((local, grid, K * groups * LANES), BF16),
        pltpu.VMEM((local, K, grid, LANES), F32),
        pltpu.VMEM(mix_one.shape, BF16),
        pltpu.VMEM(mix_one.shape, BF16),
        pltpu.VMEM(mix_two.shape, BF16),
        pltpu.VMEM(mix_two.shape, BF16),
        pltpu.VMEM(mix_nat.shape, BF16),
        pltpu.VMEM(mix_nat.shape, BF16),
        pltpu.SemaphoreType.DMA,
        pltpu.SemaphoreType.DMA((groups, n)),
        pltpu.SemaphoreType.DMA((2, groups, n)),
    ]
    macs = ITERS * 2 * rows * channels * grid * K * (grid + channels)
    return pl.pallas_call(
        functools.partial(sweep_kernel, n, quarter, q_size),
        out_shape=(
            jax.ShapeDtypeStruct(source.shape, F32),
            jax.ShapeDtypeStruct((green.shape[0], channels, grid), F32),
        ),
        in_specs=[vmem] * 6 + [pl.BlockSpec(memory_space=pl.ANY)],
        out_specs=(vmem, vmem),
        scratch_shapes=scratch,
        compiler_params=pltpu.CompilerParams(
            collective_id=0, has_side_effects=True, vmem_limit_bytes=63 * 1024 * 1024
        ),
        cost_estimate=pl.CostEstimate(
            flops=6 * macs, bytes_accessed=4 * 4 * source.size, transcendentals=0
        ),
    )(table, green_t, green, mix_one, mix_two, mix_nat, source)


def spline_matrix(
    first_index, second_index, first_weight, second_weight, first_count, second_count
):
    first_grid = jnp.arange(first_count, dtype=jnp.int32)[None, :] - first_index[:, None]
    second_grid = jnp.arange(second_count, dtype=jnp.int32)[None, :] - second_index[:, None]
    first_rows = jnp.zeros(first_grid.shape, jnp.float32)
    second_rows = jnp.zeros(second_grid.shape, jnp.float32)
    for offset in range(4):
        first_rows = first_rows + jnp.where(
            first_grid == offset, first_weight[offset][:, None], jnp.float32(0.0)
        )
        second_rows = second_rows + jnp.where(
            second_grid == offset, second_weight[offset][:, None], jnp.float32(0.0)
        )
    return (first_rows[:, :, None] * second_rows[:, None, :]).reshape(
        first_index.shape[0], first_count * second_count
    )


def class_mats(couple, row_count, start):
    classes = (start + jnp.arange(row_count, dtype=jnp.int32)) % 4
    select = jax.nn.one_hot(classes, 4, dtype=jnp.float32)
    return jnp.einsum("rc,cmn->rmn", select, couple, precision=lax.Precision.HIGHEST)


def mix(mats, values):
    return jnp.einsum("rmn,rnx->rmx", mats, values, precision=lax.Precision.HIGHEST)


def interp(values, smat):
    return jnp.einsum("rcx,yx->rcy", values, smat, precision=lax.Precision.HIGHEST)


def to_send_one(values, quarter, p_size):
    rows = values.shape[0]
    q_size = values.shape[2] // p_size
    return (
        values.reshape(rows, 4, quarter, p_size, q_size)
        .transpose(3, 1, 0, 2, 4)
        .reshape(4 * p_size, rows, quarter * q_size)
    )


def from_send_one(arrived, quarter, r_size):
    rows = arrived.shape[0]
    q_size = arrived.shape[2] // quarter
    return (
        arrived.reshape(rows, r_size, 4, quarter, q_size)
        .transpose(0, 3, 2, 4, 1)
        .reshape(rows, 4 * quarter, q_size * r_size)
    )


def to_send_two(values, quarter, r_size):
    rows = values.shape[0]
    q_size = values.shape[2] // r_size
    return (
        values.reshape(rows, quarter, 4, q_size, r_size)
        .transpose(4, 2, 0, 1, 3)
        .reshape(4 * r_size, rows, quarter * q_size)
    )


def from_send_two(arrived, quarter, p_size):
    rows = arrived.shape[0]
    q_size = arrived.shape[2] // quarter
    return (
        arrived.reshape(rows, p_size, 4, quarter, q_size)
        .transpose(0, 2, 3, 1, 4)
        .reshape(rows, 4 * quarter, p_size * q_size)
    )


def shards(
    devices,
    source,
    green,
    couple_one,
    couple_two,
    p_bracket,
    q_bracket,
    p_weight,
    q_weight,
    qr_bracket,
    r_bracket,
    qr_weight,
    r_weight,
):
    rows_one = source.shape[0]
    rows_two = green.shape[0]
    quarter = source.shape[1] // 4
    here = lax.axis_index("mom")
    p_size = rows_two * devices // 4
    r_size = rows_one * devices // 4
    q_size = source.shape[2] // p_size
    first_maps = [
        spline_matrix(p_bracket[k], q_bracket[k], p_weight[k], q_weight[k], p_size, q_size)
        for k in range(K)
    ]
    second_maps = [
        spline_matrix(qr_bracket[k], r_bracket[k], qr_weight[k], r_weight[k], q_size, r_size)
        for k in range(K)
    ]
    mats_one = [class_mats(couple_one[k], rows_one, here * rows_one) for k in range(K)]
    mats_two = [class_mats(couple_two[k], rows_two, here * rows_two) for k in range(K)]
    scale = green[:, None, :]
    state = source
    component = None
    for step in range(ITERS):
        one = interp(mix(mats_one[0], state), first_maps[0])
        k = 1
        one = one + interp(mix(mats_one[k], state), first_maps[k])
        arrived = lax.all_to_all(
            to_send_one(one, quarter, p_size), "mom", split_axis=0, concat_axis=1, tiled=True
        )
        regrouped = from_send_one(arrived, quarter, r_size)
        total = mix(mats_two[0], interp(regrouped, second_maps[0]))
        k = 1
        total = total + mix(mats_two[k], interp(regrouped, second_maps[k]))
        component = scale * total
        returned = lax.all_to_all(
            to_send_two(component, quarter, r_size), "mom", split_axis=0, concat_axis=1, tiled=True
        )
        state = source + from_send_two(returned, quarter, p_size)
    return (state, component)


def solution(mesh):
    placed = (P(("energy", "mom"), None, None), P(("energy", "mom"), None)) + (P(),) * 10
    devices = mesh.shape["mom"]

    def local_part(source, green, *rest):
        rows, channels, grid = source.shape
        block_rows = rows * LANES // 4
        fits = (
            rows == green.shape[0]
            and rows == 8
            and channels == LANES
            and grid % (2 * LANES) == 0
            and devices % (grid // (2 * LANES)) == 0
            and LANES % (grid * 4 // (rows * devices)) == 0
            and block_rows == 2 * LANES
        )
        if fits:
            return fused(devices, source, green, *rest)
        return shards(devices, source, green, *rest)

    return jax.shard_map(
        local_part,
        mesh=mesh,
        in_specs=placed,
        out_specs=(P(("energy", "mom"), None, None), P(("energy", "mom"), None, None)),
        check_vma=False,
    )
```

time: 932 us -> 499 us (0.54)
  Pallas kernels: 0 us -> 414 us
  blocking collectives: 293 us -> 0 us
  local copies, waits for them, and re-layouts: 362 us -> 80.2 us
  matrix products: 161 us -> 0 us
  waiting for transfers between devices: 84.8 us -> 0 us
  other arithmetic: 13.5 us -> 3.13 us
    pallas_call x0 -> x1, Pallas kernels: none -> 414 us  [fused(): pl.pallas_call(functools.partial(sweep_kernel, n, quarter, q_size), out_s...]
    all_to_all x3 -> x0, blocking collectives: 293 us -> none  [the longest x2 195 us: shards(): lax.all_to_all(to_send_two(component, quarter), 'mom', split_axis=0, conc...]
    reshape x20 -> x10, local copies, waits for them, and re-layouts: 271 us -> 25.2 us  [the longest x1 18.6 us: fused(): pieces = couple_two.reshape(K, groups, quarter, groups, quarter, groups)]
    dot_general x20 -> x0, matrix products: 161 us -> none  [the longest x8 120 us: interp(): jnp.einsum('rcx,yx->rcy', values, smat, precision=lax.Precision.HIGHEST)]
    all_to_all x1 -> x0, waiting for transfers between devices: 84.8 us -> none  [shards(): lax.all_to_all(to_send_one(one, quarter), 'mom', split_axis=0, concat_axi...]
    transpose x4, local copies, waits for them, and re-layouts: 74.7 us -> 29 us  [the longest x1 15.2 us: fused(): pieces.transpose(1, 0, 5, 4, 3, 2).reshape(groups, K * channels, channels)]
    broadcast_in_dim x0 -> x4, local copies, waits for them, and re-layouts: none -> 12.5 us  [fused(): jnp.where(eye, blocks[:, :, :, :, :, None, :], F32(0.0))]
    all_to_all x4 -> x0, local copies, waits for them, and re-layouts: 11.7 us -> none  [the longest x2 7.11 us: shards(): lax.all_to_all(to_send_one(one, quarter), 'mom', split_axis=0, concat_axi...]
  transfers between devices with their start and end apart: 1 -> 0, of which waited for: 1 -> 0; matrix products, arithmetic and copies ran while one was open for 1% -> 0% of each run, Pallas kernels for 0% -> 0%
where the time goes in v1:
time: 499 us; the launch traced here: 498 us
  Pallas kernels  414 us (83%)
  local copies, waits for them, and re-layouts  80.2 us (16%)
    pallas_call x1, Pallas kernels, fused(): pl.pallas_call(functools.partial(sweep_kernel, n, quarter, q_size), out_s...  414 us
    reshape x1, local copies, waits for them, and re-layouts, fused(): pieces = couple_two.reshape(K, groups, quarter, groups, quarter, groups)  18.6 us
    transpose x1, local copies, waits for them, and re-layouts, fused(): pieces.transpose(1, 0, 5, 4, 3, 2).reshape(groups, K * channels, channels)  15.2 us
    broadcast_in_dim x4, local copies, waits for them, and re-layouts, fused(): jnp.where(eye, blocks[:, :, :, :, :, None, :], F32(0.0))  12.5 us
    transpose x1, local copies, waits for them, and re-layouts, fused(): pieces.transpose(1, 2, 3, 0, 5, 4).reshape(groups, channels, K * channels)  11.1 us

profile of v1, /device:TPU:31, one launch (start us, length us, event | category | flops | bytes accessed | tf_op | source)
XLA Modules:
  0.0 497.7 jit_solution(17937363584657405546)
XLA Ops:
  0.6 0.8 slice_bitcast_fusion
  1.5 0.8 convert_reduce_fusion
  2.3 0.1 convert_element_type.99
  2.4 0.1 copy.58
  2.4 0.1 convert_element_type.101
  2.6 0.1 copy.59
  2.7 0.1 convert_element_type.105
  2.8 0.1 copy.62
  2.9 0.1 convert_element_type.109
  3.1 0.1 copy.63
  3.1 0.1 convert_element_type.113
  3.2 0.8 slice_convert_fusion
  4.0 0.7 fusion.1
  4.8 0.1 reshape_squeeze.18
  4.9 0.1 copy.64
  5.0 0.1 reshape.100
  5.1 0.7 fusion
  5.8 0.1 reshape_squeeze.19
  5.9 0.1 copy.65
  6.0 0.1 reshape.101
  6.1 0.1 reshape_squeeze.16
  6.2 0.1 copy.60
  6.2 0.1 reshape.98
  6.3 0.1 reshape_squeeze.17
  6.4 0.1 copy.61
  6.5 0.1 reshape.99
  6.6 0.4 concatenate.3
  7.0 0.2 copy.66
  7.2 0.8 pad_bitcast_fusion.tab_ref
  8.0 18.6 %reshape.104 = f32[2,4,32,4,32,4]{5,4,3,2,1,0:T(8,128)} reshape(f32[2,4,128,128]{3,2,1,0:T(8,128)S(1)} %copy-done.1) | data formatting | bytes 1048576 | tf_op jit(solution)/shard_map/reshape | solution.py:368
  26.7 15.2 %copy.70 = f32[4,2,4,32,4,32]{5,4,3,2,1,0:T(4,128)S(1)} copy(f32[4,2,4,32,4,32]{2,3,4,5,0,1:T(8,128)} %bitcast.27) | data formatting | bytes 1048576 | tf_op jit(solution)/shard_map/transpose | solution.py:369
  41.9 1.7 reshape.105.mix_two_ref
  43.5 11.1 %copy.71 = f32[4,32,4,2,4,32]{5,4,3,2,1,0:T(4,128)S(1)} copy(f32[4,32,4,2,4,32]{4,5,2,1,0,3:T(8,128)} %bitcast.28) | data formatting | bytes 1048576 | tf_op jit(solution)/shard_map/transpose | solution.py:370
  54.6 2.1 reshape.106.mix_nat_ref
  56.7 2.2 reshape.103
  59.0 1.9 copy.69
  60.9 5.0 %broadcast_in_dim.31 = f32[4,2,4,4,32,4,32]{6,5,4,3,2,1,0:T(4,128)} broadcast(f32[4,2,4,4,32,32]{5,4,3,2,1,0:T(8,128)S(1)} %copy.69), dimensions={0,1,2,3,4,6} | broadcast | bytes 2621440 | tf_op jit(solution)/shard_map/jit(_where)/broadcast_in_dim | solution.py:365
  65.9 6.5 %broadcast_in_dim.32 = f32[4,1024,128]{2,1,0:T(8,128)S(1)} reshape(f32[4,2,4,4,32,4,32]{6,5,4,3,2,1,0:T(4,128)} %broadcast_in_dim.31) | data formatting | bytes 4194304 | tf_op jit(solution)/shard_map/jit(_where)/broadcast_in_dim | solution.py:365
  72.4 0.3 broadcast_in_dim.28
  72.8 0.6 broadcast_in_dim.29
  73.4 1.5 broadcast_select_fusion.mix_one_ref
  74.9 0.1 reshape.102
  75.0 0.1 copy.67
  75.1 0.1 reshape_reshape.3
  75.2 2.0 copy.68
  77.2 413.6 %shard_map.131 = (f32[8,128,1024]{2,1,0:T(8,128)}, f32[8,128,1024]{2,1,0:T(8,128)}) custom-call(f32[1024,128]{1,0:T(8,128)} %pad_bitcast_fusion.tab_ref, f32[4,1024,2]{2,1,0:T(8,128)} %bitcast.30, f32[8,1024]{1,0:T(8,128)} %green_ref.1, f32[4,1024,128]{2,1,0:T(8,128)} %broadcast_select_fusion.mix_one_ref, f32[4,256,128]{2,1,0:T(8,128)} %reshape.105.mix_two_ref, ...), custom_call_target="tpu_custom_call" | custom-call | flops 57982058496 | bytes 16777216 | tf_op jit(solution)/shard_map/pallas_call | solution.py:396
  490.8 4.9 copy.74
  495.7 2.0 copy.75
  (12 shorter events, 0.2 us)
Async XLA Ops:
  0.6 7.4 %copy-start.1 = (f32[2,4,128,128]{3,2,1,0:T(8,128)S(1)}, f32[2,4,128,128]{3,2,1,0:T(8,128)}, u32[]{:S(2)}) copy-start(f32[2,4,128,128]{3,2,1,0:T(8,128)} %param.15) | copy-start | bytes 1572868
  54.6 2.1 copy-start.2
  73.4 1.5 copy-start.3
  490.8 5.0 copy-start

commit v2 on v1

v2 whole, which is shorter than its diff:
```python
import functools

import jax
import jax.numpy as jnp
from jax import lax
from jax.experimental import pallas as pl
from jax.experimental.pallas import tpu as pltpu
from jax.sharding import PartitionSpec as P

K = 2
ITERS = 2
LANES = 128
F32 = jnp.float32
BF16 = jnp.bfloat16


def split(values):
    high = values.astype(BF16)
    return high, (values - high.astype(F32)).astype(BF16)


def dot3(a_high, a_low, b_high, b_low, dims=(((1,), (0,)), ((), ()))):
    mul = functools.partial(lax.dot_general, dimension_numbers=dims, preferred_element_type=F32)
    return mul(a_high, b_high) + (mul(a_high, b_low) + mul(a_low, b_high))


def sweep_kernel(
    n,
    quarter,
    q_size,
    source_ref,
    green_ref,
    couple_one_ref,
    couple_two_ref,
    p_bracket_ref,
    q_bracket_ref,
    p_weight_ref,
    q_weight_ref,
    qr_bracket_ref,
    r_bracket_ref,
    qr_weight_ref,
    r_weight_ref,
    amp_ref,
    comp_ref,
    map_high,
    map_low,
    start_t,
    send_buf,
    recv_one,
    recv_two,
    v_high,
    v_low,
    w_high,
    w_low,
    w_keep,
    e_high,
    e_low,
    d_high,
    d_low,
    a_high,
    a_low,
    tab_rows,
    tab,
    tab_turned,
    square,
    load_sem,
    send_sem,
    recv_sem,
):
    me = lax.axis_index("mom")
    grid = start_t.shape[1]
    groups = start_t.shape[0]
    local = start_t.shape[2] // LANES
    block = 2 * LANES
    blocks = grid // block
    block_dests = n // blocks
    per_tile = LANES // q_size
    half = groups * LANES
    outer_size = grid // q_size

    load = pltpu.make_async_copy(source_ref, amp_ref, load_sem)
    load.start()

    def xor(left, right):
        out, unit = 0, 1
        while unit < n:
            x, y = (left // unit) % 2, (right // unit) % 2
            out = out + unit * (x + y - 2 * x * y)
            unit *= 2
        return out

    barrier = pltpu.get_barrier_semaphore()

    def greet(offset, carry):
        pl.semaphore_signal(
            barrier,
            inc=1,
            device_id={"mom": xor(me, offset)},
            device_id_type=pl.DeviceIdType.MESH,
        )
        return carry

    lax.fori_loop(1, n, greet, 0)

    def rows_of(i, size=block):
        return pl.ds(pl.multiple_of(i * size, size), size)

    tab_rows[...] = jnp.zeros_like(tab_rows)
    for k in range(K):
        for slot, refs in (
            (k, (p_bracket_ref, q_bracket_ref, p_weight_ref, q_weight_ref)),
            (K + k, (r_bracket_ref, qr_bracket_ref, r_weight_ref, qr_weight_ref)),
        ):
            at = 10 * slot
            tab_rows[at : at + 1, :] = refs[0][k : k + 1, :].astype(F32)
            tab_rows[at + 1 : at + 2, :] = refs[1][k : k + 1, :].astype(F32)
            tab_rows[at + 2 : at + 6, :] = refs[2][k]
            tab_rows[at + 6 : at + 10, :] = refs[3][k]
    green_at = 20 * K
    tab_rows[green_at : green_at + local * groups, :] = green_ref[...]
    tab[...] = tab_rows[...].T

    def build_map(slot, i, table_ref):
        base = 10 * slot
        rows = rows_of(i)
        table = table_ref[rows, :]

        def col(j):
            return jnp.broadcast_to(table[:, base + j : base + j + 1], (block, LANES))

        first, second = col(0), col(1)
        w_first = [col(2 + j) for j in range(4)]
        w_second = [col(6 + j) for j in range(4)]
        lane = lax.broadcasted_iota(jnp.int32, (block, LANES), 1)
        fine = (lane % q_size).astype(F32) - second
        coarse = (lane // q_size).astype(F32) - first
        zero = jnp.zeros((block, LANES), F32)
        inner = zero
        for j in range(4):
            inner = inner + jnp.where(fine == j, w_second[j], zero)
        for t in range(grid // LANES):
            here = coarse + F32(per_tile * t)
            outer = zero
            for j in range(4):
                outer = outer + jnp.where(here == j, w_first[j], zero)
            high, low = split(outer * inner)
            map_high[slot, rows, t * LANES : (t + 1) * LANES] = high
            map_low[slot, rows, t * LANES : (t + 1) * LANES] = low

    def copy_of(phase, g, offset):
        dest = xor(me, offset)
        into = recv_one if phase == 0 else recv_two
        return pltpu.make_async_remote_copy(
            src_ref=send_buf.at[g, dest],
            dst_ref=into.at[g, me],
            send_sem=send_sem.at[g, offset],
            recv_sem=recv_sem.at[phase, g, offset],
            device_id={"mom": dest},
            device_id_type=pl.DeviceIdType.MESH,
        )

    def keep_own(phase, g):
        into = recv_one if phase == 0 else recv_two
        into[g, me] = send_buf[g, me]

    def start_sends(phase, g):
        def body(t, carry):
            odd = t % 2
            offset = (1 - odd) * (n // 2 + t // 2) + odd * ((t + 1) // 2)
            copy_of(phase, g, offset).start()
            return carry

        lax.fori_loop(0, n - 1, body, 0)
        keep_own(phase, g)

    def start_block(phase, g, flip):
        for j in range(block_dests):
            if flip * block_dests + j > 0:
                copy_of(phase, g, flip * block_dests + j).start()

    flips = []
    for j in range(blocks // 2):
        flips += [blocks // 2 + j, (j + 1) % (blocks // 2)]

    def wait_sends(phase, g):
        def body(offset, carry):
            copy_of(phase, g, offset).wait_send()
            return carry

        lax.fori_loop(1, n, body, 0)

    def wait_recvs(phase, g):
        into = recv_one if phase == 0 else recv_two

        def body(offset, carry):
            origin = xor(me, offset)
            pltpu.make_async_remote_copy(
                src_ref=send_buf.at[g, origin],
                dst_ref=into.at[g, origin],
                send_sem=send_sem.at[g, offset],
                recv_sem=recv_sem.at[phase, g, offset],
                device_id={"mom": origin},
                device_id_type=pl.DeviceIdType.MESH,
            ).wait_recv()
            return carry

        lax.fori_loop(1, n, body, 0)

    def set_values(values):
        high, low = split(values)
        v_high[0] = high
        v_low[0] = low

    def place(g, i, part, out):
        out = out.reshape(block_dests, local, q_size, LANES)
        dests = pl.ds(i * block_dests, block_dests)
        for other in range(local):
            send_buf[
                g,
                dests,
                part * q_size : (part + 1) * q_size,
                other * LANES : (other + 1) * LANES,
            ] = out[:, other]

    def mix_first(g):
        def body(i, carry):
            rows = rows_of(i)
            e_both = [
                jnp.concatenate([ref[g, k * half : (k + 1) * half, :] for k in range(K)], axis=1)
                for ref in (e_high, e_low)
            ]
            for part in range(local):
                lanes = slice(part * LANES, (part + 1) * LANES)
                joined = jnp.concatenate([start_t[c, rows, lanes] for c in range(groups)], axis=1)
                high, low = split(joined)
                high, low = split(dot3(high, low, *e_both))
                for k in range(K):
                    v_high[k, rows, lanes] = high[:, k * LANES : (k + 1) * LANES]
                    v_low[k, rows, lanes] = low[:, k * LANES : (k + 1) * LANES]
            return carry

        lax.fori_loop(0, blocks, body, 0)

    def first_rows(g, i):
        rows = rows_of(i)
        out = sum(
            dot3(map_high[k, rows, :], map_low[k, rows, :], v_high[k], v_low[k]) for k in range(K)
        )
        for part in range(local):
            place(g, i, part, out[:, part * LANES : (part + 1) * LANES])

    def interp_one(g, i):
        rows = rows_of(i)
        for k in range(K):
            out = dot3(map_high[k, rows, :], map_low[k, rows, :], v_high[0], v_low[0])
            high, low = split(out)
            lanes = pl.ds(pl.multiple_of((k * groups + g) * LANES, LANES), LANES)
            for part in range(local):
                w_high[part, rows, lanes] = high[:, part * LANES : (part + 1) * LANES]
                w_low[part, rows, lanes] = low[:, part * LANES : (part + 1) * LANES]

    def mix_one(g, i):
        rows = rows_of(i)
        for part in range(local):
            out = dot3(w_high[part, rows, :], w_low[part, rows, :], e_high[g], e_low[g])
            place(g, i, part, out)

    def each_block(work):
        def body(i, carry):
            work(i)
            return carry

        lax.fori_loop(0, blocks, body, 0)

    def each_group(first, last, work):
        def body(g, carry):
            work(g)
            return carry

        lax.fori_loop(first, last, body, 0)

    def one(it):
        if it == 0:
            mix_first(0)
            pl.semaphore_wait(barrier, n - 1)
        else:

            def arrive(g):
                wait_recvs(1, g)
                set_values(start_t[g] + recv_two[g].reshape(grid, local * LANES))

            def take(g):
                arrive(g)
                each_block(functools.partial(interp_one, g))

            each_group(0, groups - 1, take)
            arrive(groups - 1)
            wait_sends(1, 0)
        for flip in flips:
            i = xor(me // block_dests, flip)
            if it == 0:
                for k in range(K):
                    build_map(k, i, tab)
                first_rows(0, i)
            else:
                interp_one(groups - 1, i)
                mix_one(0, i)
            start_block(0, 0, flip)
        keep_own(0, 0)

        def give(g):
            if it == 0:
                mix_first(g)
                each_block(functools.partial(first_rows, g))
            else:
                wait_sends(1, g)
                each_block(functools.partial(mix_one, g))
            start_sends(0, g)

        each_group(1, groups, give)

    def two(it):
        last = it == ITERS - 1

        def work(g):
            wait_recvs(0, g)
            wait_sends(0, g)
            set_values(recv_one[g].reshape(grid, local * LANES))

            def rows_body(i):
                rows = rows_of(i)
                outs = [
                    dot3(map_high[K + k, rows, :], map_low[K + k, rows, :], v_high[0], v_low[0])
                    for k in range(K)
                ]
                table = tab_turned[rows, :]
                lane = lax.broadcasted_iota(jnp.int32, table.shape, 1)
                for part in range(local):
                    lanes = slice(part * LANES, (part + 1) * LANES)
                    high, low = split(jnp.concatenate([out[:, lanes] for out in outs], axis=1))
                    mixed = dot3(high, low, d_high[g], d_low[g])
                    here = lane == green_at + part * groups + g
                    scale = jnp.sum(jnp.where(here, table, F32(0.0)), axis=1, keepdims=True)
                    place(g, i, part, mixed * scale)
                    if last:
                        for k in range(K):
                            w_keep[part, k, rows, :] = outs[k][:, lanes]

            each_block(rows_body)
            start_sends(1, g)
            if last:
                step = block // outer_size
                for part in range(local):
                    scale = green_ref[pl.ds(part * groups + g, 1), :]
                    for s in range(blocks):
                        joined = jnp.concatenate(
                            [
                                jnp.concatenate(
                                    [
                                        w_keep[part, k, pl.ds(q, outer_size, stride=q_size), :]
                                        for q in range(s * step, (s + 1) * step)
                                    ],
                                    axis=0,
                                )
                                for k in range(K)
                            ],
                            axis=1,
                        )
                        high, low = split(joined)
                        out = dot3(a_high[g], a_low[g], high, low, (((1,), (1,)), ((), ())))
                        lanes = slice(s * block, (s + 1) * block)
                        comp_ref[part * groups + g, :, lanes] = out * scale[:, lanes]

        each_group(0, groups, work)

    lane = lax.broadcasted_iota(jnp.int32, (LANES, LANES), 1)
    for k in range(K):
        for c in range(groups):
            turned = couple_one_ref[k, c].T
            for to in range(groups):
                shift = ((c - to) * quarter) % LANES
                moved = pltpu.roll(turned, shift, 1) if shift else turned
                high, low = split(jnp.where(lane // quarter == c, moved, F32(0.0)))
                for g in range(groups):
                    at = (k * groups + g) * LANES + c * quarter
                    e_high[to, at : at + quarter, :] = high[g * quarter : (g + 1) * quarter]
                    e_low[to, at : at + quarter, :] = low[g * quarter : (g + 1) * quarter]
    load.wait()

    def transpose_in(g):
        chans = pl.ds(pl.multiple_of(g * quarter, quarter), quarter)
        for part in range(local):
            stacked = jnp.concatenate(
                [amp_ref[part * groups + c, chans, :] for c in range(groups)], axis=0
            )
            start_t[g, :, part * LANES : (part + 1) * LANES] = stacked.T

    each_group(0, groups, transpose_in)
    one(0)

    for r in range(outer_size):
        tab_turned[r * q_size : (r + 1) * q_size, :] = tab[pl.ds(r, q_size, stride=outer_size), :]

    def build_two(i):
        for k in range(K):
            build_map(K + k, i, tab_turned)

    each_block(build_two)

    def picked(load):
        return jnp.concatenate(
            [load(pl.ds(c, quarter, stride=groups)) for c in range(groups)], axis=0
        )

    def couple(g):
        for k in range(K):
            square[...] = picked(lambda rows: couple_two_ref[k, g, rows, :]).T
            high, low = split(picked(lambda rows: square[rows, :]))
            d_high[g, k * LANES : (k + 1) * LANES, :] = high
            d_low[g, k * LANES : (k + 1) * LANES, :] = low
            square[...] = couple_two_ref[k, g].T
            high, low = split(picked(lambda rows: square[rows, :]).T)
            a_high[g, :, k * LANES : (k + 1) * LANES] = high
            a_low[g, :, k * LANES : (k + 1) * LANES] = low

    each_group(0, groups, couple)
    two(0)
    for it in range(1, ITERS):
        one(it)
        two(it)

    def finish(g):
        wait_recvs(1, g)
        total = start_t[g] + recv_two[g].reshape(grid, local * LANES)
        chans = pl.ds(pl.multiple_of(g * quarter, quarter), quarter)
        for part in range(local):
            turned = total[:, part * LANES : (part + 1) * LANES].T
            for c in range(groups):
                amp_ref[part * groups + c, chans, :] = turned[c * quarter : (c + 1) * quarter]
        wait_sends(1, g)

    each_group(0, groups, finish)


def fused(n, source, green, couple_one, couple_two, *tables):
    rows, channels, grid = source.shape
    groups = couple_one.shape[1]
    quarter = channels // groups
    local = rows // groups
    q_size = grid // (rows * n // groups)

    vmem = pl.BlockSpec(memory_space=pltpu.VMEM)
    boxes = (groups, n, local * q_size, local * LANES)
    scratch = [
        pltpu.VMEM((2 * K, grid, grid), BF16),
        pltpu.VMEM((2 * K, grid, grid), BF16),
        pltpu.VMEM((groups, grid, local * LANES), F32),
        pltpu.VMEM(boxes, F32),
        pltpu.VMEM(boxes, F32),
        pltpu.VMEM(boxes, F32),
        pltpu.VMEM((K, grid, local * LANES), BF16),
        pltpu.VMEM((K, grid, local * LANES), BF16),
        pltpu.VMEM((local, grid, K * groups * LANES), BF16),
        pltpu.VMEM((local, grid, K * groups * LANES), BF16),
        pltpu.VMEM((local, K, grid, LANES), F32),
        pltpu.VMEM((groups, K * groups * LANES, LANES), BF16),
        pltpu.VMEM((groups, K * groups * LANES, LANES), BF16),
        pltpu.VMEM((groups, K * LANES, LANES), BF16),
        pltpu.VMEM((groups, K * LANES, LANES), BF16),
        pltpu.VMEM((groups, LANES, K * LANES), BF16),
        pltpu.VMEM((groups, LANES, K * LANES), BF16),
        pltpu.VMEM((LANES, grid), F32),
        pltpu.VMEM((grid, LANES), F32),
        pltpu.VMEM((grid, LANES), F32),
        pltpu.VMEM((LANES, LANES), F32),
        pltpu.SemaphoreType.DMA,
        pltpu.SemaphoreType.DMA((groups, n)),
        pltpu.SemaphoreType.DMA((2, groups, n)),
    ]
    macs = ITERS * 2 * rows * channels * grid * K * (grid + channels)
    return pl.pallas_call(
        functools.partial(sweep_kernel, n, quarter, q_size),
        out_shape=(
            jax.ShapeDtypeStruct(source.shape, F32),
            jax.ShapeDtypeStruct((green.shape[0], channels, grid), F32),
        ),
        in_specs=[pl.BlockSpec(memory_space=pl.ANY)] + [vmem] * (3 + len(tables)),
        out_specs=(vmem, vmem),
        scratch_shapes=scratch,
        compiler_params=pltpu.CompilerParams(
            collective_id=0, has_side_effects=True, vmem_limit_bytes=63 * 1024 * 1024
        ),
        cost_estimate=pl.CostEstimate(
            flops=6 * macs, bytes_accessed=4 * 4 * source.size, transcendentals=0
        ),
    )(source, green, couple_one, couple_two, *tables)


def spline_matrix(
    first_index, second_index, first_weight, second_weight, first_count, second_count
):
    first_grid = jnp.arange(first_count, dtype=jnp.int32)[None, :] - first_index[:, None]
    second_grid = jnp.arange(second_count, dtype=jnp.int32)[None, :] - second_index[:, None]
    first_rows = jnp.zeros(first_grid.shape, jnp.float32)
    second_rows = jnp.zeros(second_grid.shape, jnp.float32)
    for offset in range(4):
        first_rows = first_rows + jnp.where(
            first_grid == offset, first_weight[offset][:, None], jnp.float32(0.0)
        )
        second_rows = second_rows + jnp.where(
            second_grid == offset, second_weight[offset][:, None], jnp.float32(0.0)
        )
    return (first_rows[:, :, None] * second_rows[:, None, :]).reshape(
        first_index.shape[0], first_count * second_count
    )


def class_mats(couple, row_count, start):
    classes = (start + jnp.arange(row_count, dtype=jnp.int32)) % 4
    select = jax.nn.one_hot(classes, 4, dtype=jnp.float32)
    return jnp.einsum("rc,cmn->rmn", select, couple, precision=lax.Precision.HIGHEST)


def mix(mats, values):
    return jnp.einsum("rmn,rnx->rmx", mats, values, precision=lax.Precision.HIGHEST)


def interp(values, smat):
    return jnp.einsum("rcx,yx->rcy", values, smat, precision=lax.Precision.HIGHEST)


def to_send_one(values, quarter, p_size):
    rows = values.shape[0]
    q_size = values.shape[2] // p_size
    return (
        values.reshape(rows, 4, quarter, p_size, q_size)
        .transpose(3, 1, 0, 2, 4)
        .reshape(4 * p_size, rows, quarter * q_size)
    )


def from_send_one(arrived, quarter, r_size):
    rows = arrived.shape[0]
    q_size = arrived.shape[2] // quarter
    return (
        arrived.reshape(rows, r_size, 4, quarter, q_size)
        .transpose(0, 3, 2, 4, 1)
        .reshape(rows, 4 * quarter, q_size * r_size)
    )


def to_send_two(values, quarter, r_size):
    rows = values.shape[0]
    q_size = values.shape[2] // r_size
    return (
        values.reshape(rows, quarter, 4, q_size, r_size)
        .transpose(4, 2, 0, 1, 3)
        .reshape(4 * r_size, rows, quarter * q_size)
    )


def from_send_two(arrived, quarter, p_size):
    rows = arrived.shape[0]
    q_size = arrived.shape[2] // quarter
    return (
        arrived.reshape(rows, p_size, 4, quarter, q_size)
        .transpose(0, 2, 3, 1, 4)
        .reshape(rows, 4 * quarter, p_size * q_size)
    )


def shards(
    devices,
    source,
    green,
    couple_one,
    couple_two,
    p_bracket,
    q_bracket,
    p_weight,
    q_weight,
    qr_bracket,
    r_bracket,
    qr_weight,
    r_weight,
):
    rows_one = source.shape[0]
    rows_two = green.shape[0]
    quarter = source.shape[1] // 4
    here = lax.axis_index("mom")
    p_size = rows_two * devices // 4
    r_size = rows_one * devices // 4
    q_size = source.shape[2] // p_size
    first_maps = [
        spline_matrix(p_bracket[k], q_bracket[k], p_weight[k], q_weight[k], p_size, q_size)
        for k in range(K)
    ]
    second_maps = [
        spline_matrix(qr_bracket[k], r_bracket[k], qr_weight[k], r_weight[k], q_size, r_size)
        for k in range(K)
    ]
    mats_one = [class_mats(couple_one[k], rows_one, here * rows_one) for k in range(K)]
    mats_two = [class_mats(couple_two[k], rows_two, here * rows_two) for k in range(K)]
    scale = green[:, None, :]
    state = source
    component = None
    for step in range(ITERS):
        one = interp(mix(mats_one[0], state), first_maps[0])
        k = 1
        one = one + interp(mix(mats_one[k], state), first_maps[k])
        arrived = lax.all_to_all(
            to_send_one(one, quarter, p_size), "mom", split_axis=0, concat_axis=1, tiled=True
        )
        regrouped = from_send_one(arrived, quarter, r_size)
        total = mix(mats_two[0], interp(regrouped, second_maps[0]))
        k = 1
        total = total + mix(mats_two[k], interp(regrouped, second_maps[k]))
        component = scale * total
        returned = lax.all_to_all(
            to_send_two(component, quarter, r_size), "mom", split_axis=0, concat_axis=1, tiled=True
        )
        state = source + from_send_two(returned, quarter, p_size)
    return (state, component)


def solution(mesh):
    placed = (P(("energy", "mom"), None, None), P(("energy", "mom"), None)) + (P(),) * 10
    devices = mesh.shape["mom"]

    def local_part(source, green, *rest):
        rows, channels, grid = source.shape
        block_rows = rows * LANES // 4
        fits = (
            rows == green.shape[0]
            and rows == 8
            and channels == LANES
            and grid % (2 * LANES) == 0
            and grid // (2 * LANES) in (2, 4, 8, 16)
            and devices in (8, 16, 32, 64)
            and devices % (grid // (2 * LANES)) == 0
            and LANES % (grid * 4 // (rows * devices)) == 0
            and block_rows == 2 * LANES
        )
        if fits:
            return fused(devices, source, green, *rest)
        return shards(devices, source, green, *rest)

    return jax.shard_map(
        local_part,
        mesh=mesh,
        in_specs=placed,
        out_specs=(P(("energy", "mom"), None, None), P(("energy", "mom"), None, None)),
        check_vma=False,
    )
```

time: 499 us -> 390 us (0.78)
  local copies, waits for them, and re-layouts: 80.2 us -> 6.96 us
  Pallas kernels: 414 us -> 377 us
    pallas_call x1, Pallas kernels: 414 us -> 377 us  [fused(): pl.pallas_call(functools.partial(sweep_kernel, n, quarter, q_size), out_s...]
    transpose x4 -> x0, local copies, waits for them, and re-layouts: 29 us -> none  [the longest x1 15.2 us: fused(): pieces.transpose(1, 0, 5, 4, 3, 2).reshape(groups, K * channels, channels)]
    reshape x10 -> x0, local copies, waits for them, and re-layouts: 25.2 us -> none  [the longest x1 18.6 us: fused(): pieces = couple_two.reshape(K, groups, quarter, groups, quarter, groups)]
    broadcast_in_dim x4 -> x0, local copies, waits for them, and re-layouts: 12.5 us -> none  [fused(): jnp.where(eye, blocks[:, :, :, :, :, None, :], F32(0.0))]
where the time goes in v2:
time: 390 us; the launch traced here: 384 us
  Pallas kernels  377 us (97%)
  local copies, waits for them, and re-layouts  6.96 us (2%)
    pallas_call x1, Pallas kernels, fused(): pl.pallas_call(functools.partial(sweep_kernel, n, quarter, q_size), out_s...  377 us

profile of v2, /device:TPU:31, one launch (start us, length us, event | category | flops | bytes accessed | tf_op | source)
XLA Modules:
  0.0 384.3 jit_solution(18144066066508202911)
XLA Ops:
  0.6 376.7 %shard_map.131 = (f32[8,128,1024]{2,1,0:T(8,128)}, f32[8,128,1024]{2,1,0:T(8,128)}) custom-call(f32[8,128,1024]{2,1,0:T(8,128)} %source_ref.1, f32[8,1024]{1,0:T(8,128)} %green_ref.1, f32[2,4,128,128]{3,2,1,0:T(8,128)} %couple_one_ref.1, f32[2,4,128,128]{3,2,1,0:T(8,128)} %couple_two_ref.1, s32[2,1024]{1,0:T(2,128)} %p_bracket_ref.1, ...), custom_call_target="tpu_custom_call" | custom-call | flops 57982058496 | bytes 16777216 | tf_op jit(solution)/shard_map/pallas_call | solution.py:481
  377.3 0.0 copy-start
  377.3 4.9 %copy.16 = f32[8,128,1024]{2,1,0:T(8,128)} copy(f32[8,128,1024]{2,1,0:T(8,128)} %get-tuple-element.4) | data formatting | bytes 8388608
  382.3 0.0 copy-done
  382.3 2.0 copy.17
Async XLA Ops:
  377.3 5.0 %copy-start = (f32[8,128,1024]{2,1,0:T(8,128)S(1)}, f32[8,128,1024]{2,1,0:T(8,128)}, u32[]{:S(2)}) copy-start(f32[8,128,1024]{2,1,0:T(8,128)} %get-tuple-element.5) | copy-start | bytes 12582916
